TPU v7x, 32 devices: a whole 2x2x4 slice. The times are simulated.
32 devices in a mesh: lst: 4 (over y, x), night: 8 (over z, core).
Axes of the slice: x: 2, y: 2, z: 4, core: 2. Of those that a mesh axis runs over, the one named last changes fastest.
Arguments:
- visibility: bfloat16 [8, 32, 16, 2, 1536], P('night', 'lst'), may hold values from -18 to 18
- flags: int32 [8, 32, 16, 1536], P('night', 'lst'), may hold values 0 or 1
- counts: int32 [8, 32], P('night', 'lst'), may hold values from 1 to 4
- offsets: int32 [8], P('night'), may hold values from -6 to 6, as said below
- fraction: float32 [8], P('night'), may hold values from 0 to 1
- gains: float32 [8, 2, 1536], P('night'), may hold values from -6 to 6
- inverse_var: float32 [8, 1536], P('night'), may hold values from 0.005 to 0.05
- prior: float32 [1536], replicated, may hold values from 0.5 to 5
Outputs:
- binned: bfloat16 [32, 16, 2, 1536], P('lst')
- weight_total: float32 [32, 16, 1536], P('lst')
Inputs may be any that keep to these rules, and one draw needn't show every extreme that they name: `offsets`: both -6 and 6 occur among the nights.
All inputs are finite; a program needn't handle non-finite values. No bound on the sum of `flags` on one device may be relied on, other than what follows from the above.
Results may differ from a plain program's by a relative error of at most 0.009.
Values may be sent and summed in bfloat16 or wider, within the bound.
A program may use at most 64 MiB of HBM per device.

v0:
```python
import jax
import jax.numpy as jnp
from jax import lax
from jax.sharding import PartitionSpec as P


def extended(x, sides, width):
    for axis, dim in sides:
        size, length = (lax.axis_size(axis), x.shape[dim])
        up = [(i, (i + 1) % size) for i in range(size)]
        down = [(j, i) for i, j in up]
        last = lax.slice_in_dim(x, length - width, length, axis=dim)
        first = lax.slice_in_dim(x, 0, width, axis=dim)
        before = lax.ppermute(last, axis, up)
        after = lax.ppermute(first, axis, down)
        x = jnp.concatenate([before, x, after], axis=dim)
    return x


def spline_taps(fraction):
    cube = fraction * fraction * fraction
    square = fraction * fraction
    first = (1.0 - fraction) ** 3 / 6.0
    second = (3.0 * cube - 6.0 * square + 4.0) / 6.0
    third = (-3.0 * cube + 3.0 * square + 3.0 * fraction + 1.0) / 6.0
    fourth = cube / 6.0
    return jnp.stack([first, second, third, fourth], axis=-1)


def shards(visibility, flags, counts, offsets, fraction, gains, inverse_var, prior):
    local_nights = visibility.shape[0]
    sample_count = visibility.shape[1]
    baseline_count = visibility.shape[2]
    channel_count = visibility.shape[4]
    scale = (flags * counts[:, :, None, None]).astype(jnp.float32) * inverse_var[:, None, None, :]
    weight = scale.astype(jnp.bfloat16)
    real_part = visibility[:, :, :, 0].astype(jnp.float32)
    imag_part = visibility[:, :, :, 1].astype(jnp.float32)
    gain_re = gains[:, 0][:, None, None, :]
    gain_im = gains[:, 1][:, None, None, :]
    cal_re = gain_re * real_part - gain_im * imag_part
    cal_im = gain_re * imag_part + gain_im * real_part
    weighted = (scale[:, :, :, None, :] * jnp.stack([cal_re, cal_im], axis=3)).astype(jnp.bfloat16)
    stacked = jnp.concatenate([weighted, weight[:, :, :, None, :]], axis=3)
    taps = spline_taps(fraction)
    tap_index = jnp.arange(4).reshape(1, 1, 1, 4)
    shifts = offsets.reshape(1, local_nights, 1, 1)
    tap_values = taps.reshape(1, local_nights, 1, 4)
    padded_slab = extended(stacked, (("lst", 1),), sample_count)
    out_row = jnp.arange(sample_count).reshape(sample_count, 1, 1, 1)
    source = jnp.arange(3 * sample_count).reshape(1, 1, 3 * sample_count, 1)
    target = out_row - shifts + tap_index - 1 + sample_count
    matrix = jnp.sum(jnp.where(source == target, tap_values, 0.0), axis=-1).astype(jnp.bfloat16)
    partial_numerator = jnp.dot(
        matrix.reshape(sample_count, local_nights * 3 * sample_count),
        padded_slab.reshape(local_nights * 3 * sample_count, baseline_count * 3 * channel_count),
        preferred_element_type=jnp.float32,
    )
    partial_numerator = partial_numerator.reshape(sample_count, baseline_count, 3, channel_count)
    totals = lax.psum(partial_numerator, "night")
    denominator_sum = totals[:, :, 2]
    binned = (
        totals[:, :, 0:2] / (denominator_sum[:, :, None, :] + prior[None, None, None, :])
    ).astype(jnp.bfloat16)
    return (binned, denominator_sum)


def solution(mesh):
    in_specs = (
        P("night", "lst", None, None, None),
        P("night", "lst", None, None),
        P("night", "lst"),
        P("night"),
        P("night"),
        P("night", None, None),
        P("night", None),
        P(),
    )
    out_specs = (P("lst", None, None, None), P("lst", None, None))
    return jax.shard_map(shards, mesh=mesh, in_specs=in_specs, out_specs=out_specs, check_vma=False)
```

profile of v0, /device:TPU:0, one launch (start us, length us, event | category | flops | bytes accessed | tf_op | source)
XLA Modules:
  0.0 172.8 jit_solution(5491326670959882846)
XLA Ops:
  7.2 0.0 copy-start.3
  7.2 0.0 copy-start.1
  7.2 0.0 copy-start.4
  7.2 0.0 all-reduce.2.cloned.1.call-start
  7.2 0.8 slice_reduce_fusion.1
  8.1 3.0 %fusion.11 = (bf16[1,8,16,1,1536]{4,3,2,1,0:T(2,128)(2,1)S(1)}, bf16[1,8,16,1,1536]{4,3,2,1,0:T(2,128)(2,1)S(1)}) fusion(bf16[1,8,16,2,1536]{4,3,2,1,0:T(2,128)(2,1)} %param.8), kind=kLoop, calls=%fused_computation.29 | loop fusion | bytes 1572864 | tf_op jit(solution)/shard_map/slice | solution.py:37
  11.1 0.0 copy-done.3
  11.2 0.0 copy-done.1
  11.2 0.0 copy-done.4
  11.2 0.2 fusion.7
  11.4 0.3 fusion.4
  11.7 0.1 fusion.3
  11.8 0.1 pad_maximum_fusion.1
  11.9 3.9 %collective-permute-start.1 = (bf16[1,8,16,3,1536]{4,2,3,1,0:T(8,128)(2,1)S(1)}, bf16[1,8,16,3,1536]{4,2,3,1,0:T(8,128)(2,1)S(1)}, u32[]{:S(2)}, u32[]{:S(2)}) collective-permute-start(bf16[1,8,16,3,1536]{4,2,3,1,0:T(8,128)(2,1)S(1)} %pad_maximum_fusion.1), channel_id=1, source_target_pairs={{8,0},{16,8},{24,16},{0,24},{9,1},{17,9},{25,17},{1,25},{10,2},{18... | collective-permute-start | bytes 3538952 | tf_op jit(solution)/shard_map/ppermute | solution.py:15
  15.9 0.0 collective-permute-start
  17.2 0.1 maximum_bitcast_fusion
  17.3 0.1 select_reduce_fusion
  17.4 24.9 %collective-permute-done.1 = bf16[1,8,16,3,1536]{4,2,3,1,0:T(8,128)(2,1)S(1)} collective-permute-done((bf16[1,8,16,3,1536]{4,2,3,1,0:T(8,128)(2,1)S(1)}, bf16[1,8,16,3,1536]{4,2,3,1,0:T(8,128)(2,1)S(1)}, u32[]{:S(2)}, u32[]{:S(2)}) %collective-permute-start.1) | collective-permute-done | bytes 1179680 | tf_op jit(solution)/shard_map/ppermute | solution.py:15
  42.3 25.1 %collective-permute-done = bf16[1,8,16,3,1536]{4,2,3,1,0:T(8,128)(2,1)S(1)} collective-permute-done((bf16[1,8,16,3,1536]{4,2,3,1,0:T(8,128)(2,1)S(1)}, bf16[1,8,16,3,1536]{4,2,3,1,0:T(8,128)(2,1)S(1)}, u32[]{:S(2)}, u32[]{:S(2)}) %collective-permute-start) | collective-permute-done | bytes 1179680 | tf_op jit(solution)/shard_map/ppermute | solution.py:14
  67.4 0.4 pad_maximum_fusion
  67.8 5.4 %copy.25 = bf16[1,24,16,3,1536]{4,3,2,1,0:T(4,128)(2,1)} copy(bf16[1,24,16,3,1536]{4,2,3,1,0:T(8,128)(2,1)S(1)} %pad_maximum_fusion) | data formatting | bytes 7077888 | tf_op jit(solution)/shard_map/concatenate | solution.py:16
  73.2 6.2 %reshape.136 = bf16[24,73728]{1,0:T(8,128)(2,1)S(1)} reshape(bf16[1,24,16,3,1536]{4,3,2,1,0:T(4,128)(2,1)} %copy.25) | data formatting | bytes 7077888 | tf_op jit(solution)/shard_map/reshape | solution.py:56
  79.4 6.2 %dot_general.8 = bf16[16,3,1536,24]{2,1,0,3:T(4,128)(2,1)} reshape(bf16[73728,24]{0,1:T(8,128)(2,1)S(1)} %bitcast.25) | data formatting | bytes 7077888 | tf_op jit(solution)/shard_map/dot_general | solution.py:54
  85.6 8.3 %fusion = f32[8,16,3,1536]{3,0,2,1:T(8,128)} fusion(bf16[16,3,1536,24]{2,1,0,3:T(4,128)(2,1)} %dot_general.8, bf16[8,24]{1,0:T(8,128)(2,1)S(1)} %select_reduce_fusion), kind=kOutput, calls=%fused_computation.1 | convolution fusion | flops 28311552 | bytes 5898624 | tf_op jit(solution)/shard_map/dot_general | solution.py:54
  93.8 0.0 all-reduce.2.cloned.1.call-update
  93.9 67.2 %all-reduce.2.cloned.1.call-done = f32[8,16,3,1536]{3,0,2,1:T(8,128)} async-done(((f32[8,16,3,1536]{3,0,2,1:T(8,128)}), f32[8,16,3,1536]{3,0,2,1:T(8,128)}) %all-reduce.2.cloned.1.call-update) | async-done | bytes 2359312 | tf_op jit(solution)/shard_map/psum | solution.py:60
  161.0 0.0 copy-done.2
  161.0 1.4 slice_bitcast_fusion
  162.5 0.4 copy-done
  162.9 0.2 fusion.2
  163.1 1.5 copy.27
  164.6 1.3 copy.28
  (5 shorter events, 0.0 us)
Async XLA Ops:
  7.2 4.0 %copy-start.3 = (f32[1,1536]{1,0:T(1,128)S(1)}, f32[1,1536]{1,0:T(1,128)}, u32[]{:S(2)}) copy-start(f32[1,1536]{1,0:T(1,128)} %param.14) | copy-start | bytes 18436
  7.2 4.0 %copy-start.1 = (s32[1,8,16,1536]{3,2,1,0:T(8,128)S(1)}, s32[1,8,16,1536]{3,2,1,0:T(8,128)}, u32[]{:S(2)}) copy-start(s32[1,8,16,1536]{3,2,1,0:T(8,128)} %param.9) | copy-start | bytes 2359300
  7.2 4.0 %copy-start.4 = (s32[1,8]{1,0:T(1,128)S(1)}, s32[1,8]{1,0:T(1,128)}, u32[]{:S(2)}) copy-start(s32[1,8]{1,0:T(1,128)} %param.10) | copy-start | bytes 100
  7.2 153.8 %all-reduce.2.cloned.1.call-start = ((), (), s32[]{:S(2)}) async-start(), calls=%async_computation | async-start | bytes 4718592 | tf_op jit(solution)/shard_map/psum | solution.py:60
  11.9 30.3 %collective-permute-start.1 = (bf16[1,8,16,3,1536]{4,2,3,1,0:T(8,128)(2,1)S(1)}, bf16[1,8,16,3,1536]{4,2,3,1,0:T(8,128)(2,1)S(1)}, u32[]{:S(2)}, u32[]{:S(2)}) collective-permute-start(bf16[1,8,16,3,1536]{4,2,3,1,0:T(8,128)(2,1)S(1)} %pad_maximum_fusion.1), channel_id=1, source_target_pairs={{8,0},{16,8},{24,16},{0,24},{9,1},{17,9},{25,17},{1,25},{10,2},{18... | collective-permute-start | bytes 3538952 | tf_op jit(solution)/shard_map/ppermute | solution.py:15
  15.9 51.5 %collective-permute-start = (bf16[1,8,16,3,1536]{4,2,3,1,0:T(8,128)(2,1)S(1)}, bf16[1,8,16,3,1536]{4,2,3,1,0:T(8,128)(2,1)S(1)}, u32[]{:S(2)}, u32[]{:S(2)}) collective-permute-start(bf16[1,8,16,3,1536]{4,2,3,1,0:T(8,128)(2,1)S(1)} %pad_maximum_fusion.1), channel_id=1, source_target_pairs={{0,8},{8,16},{16,24},{24,0},{1,9},{9,17},{17,25},{25,1},{2,10},{10... | collective-permute-start | bytes 3538952 | tf_op jit(solution)/shard_map/ppermute | solution.py:14
  93.8 67.2 %copy-start.2 = (f32[1536]{0:T(1024)S(1)}, f32[1536]{0:T(1024)}, u32[]{:S(2)}) copy-start(f32[1536]{0:T(1024)} %param.15) | copy-start | bytes 18436
  161.0 1.9 %copy-start = (f32[8,16,3,1536]{3,0,2,1:T(8,128)S(1)}, f32[8,16,3,1536]{3,0,2,1:T(8,128)}, u32[]{:S(2)}) copy-start(f32[8,16,3,1536]{3,0,2,1:T(8,128)} %all-reduce.2.cloned.1.call-done) | copy-start | bytes 7077892
Sparse Core Ops, SparseCore 0:
  94.0 67.0 all-reduce.1
where the time goes:
time: 173 us
  waiting for transfers between devices  117 us (68%)
  local copies, waits for them, and re-layouts  24.9 us (14%)
  between operations  15.5 us (9%)
  matrix products  8.26 us (5%)
  starting transfers between devices  3.99 us (2%)
  other arithmetic  2.95 us (2%)
    psum x1, waiting for transfers between devices, shards(): totals = lax.psum(partial_numerator, 'night')  67.2 us
    ppermute x1, waiting for transfers between devices, extended(): before = lax.ppermute(last, axis, up)  25.1 us
    ppermute x1, waiting for transfers between devices, extended(): after = lax.ppermute(first, axis, down)  24.9 us
    dot_general x1, matrix products, shards(): jnp.dot(matrix.reshape(sample_count, local_nights * 3 * sample_count), pa...  8.26 us
    dot_general x1, local copies, waits for them, and re-layouts, shards(): jnp.dot(matrix.reshape(sample_count, local_nights * 3 * sample_count), pa...  6.2 us
    reshape x1, local copies, waits for them, and re-layouts, shards(): padded_slab.reshape(local_nights * 3 * sample_count, baseline_count * 3 *...  6.2 us
    concatenate x1, local copies, waits for them, and re-layouts, extended(): x = jnp.concatenate([before, x, after], axis=dim)  5.36 us
    ppermute x1, starting transfers between devices, extended(): after = lax.ppermute(first, axis, down)  3.95 us
  transfers between devices with their start and end apart: 3, of which 3 were waited for; matrix products, arithmetic and copies ran while one was open for 0% of the time, Pallas kernels for 0%

commit v1 on v0

--- a/solution.py
+++ b/solution.py
@@ -57,7 +57,7 @@
         preferred_element_type=jnp.float32,
     )
     partial_numerator = partial_numerator.reshape(sample_count, baseline_count, 3, channel_count)
-    totals = lax.psum(partial_numerator, "night")
+    totals = jnp.sum(lax.all_gather(partial_numerator, "night"), axis=0)
     denominator_sum = totals[:, :, 2]
     binned = (
         totals[:, :, 0:2] / (denominator_sum[:, :, None, :] + prior[None, None, None, :])

time: 173 us -> 282 us (1.63)
  waiting for transfers between devices: 117 us -> 219 us
  other arithmetic: 2.95 us -> 10.7 us
    all_gather x0 -> x1, waiting for transfers between devices: none -> 169 us  [shards(): totals = jnp.sum(lax.all_gather(partial_numerator, 'night'), axis=0)]
    psum x1 -> x0, waiting for transfers between devices: 67.2 us -> none  [shards(): totals = lax.psum(partial_numerator, 'night')]
    reduce_sum x0 -> x1, other arithmetic: none -> 8.94 us  [shards(): totals = jnp.sum(lax.all_gather(partial_numerator, 'night'), axis=0)]
where the time goes in v1:
time: 282 us
  waiting for transfers between devices  219 us (78%)
  local copies, waits for them, and re-layouts  24.4 us (9%)
  between operations  15.5 us (5%)
  other arithmetic  10.7 us (4%)
  matrix products  8.22 us (3%)
  starting transfers between devices  3.99 us (1%)
    all_gather x1, waiting for transfers between devices, shards(): totals = jnp.sum(lax.all_gather(partial_numerator, 'night'), axis=0)  169 us
    ppermute x1, waiting for transfers between devices, extended(): before = lax.ppermute(last, axis, up)  25.1 us
    ppermute x1, waiting for transfers between devices, extended(): after = lax.ppermute(first, axis, down)  24.9 us
    reduce_sum x1, other arithmetic, shards(): totals = jnp.sum(lax.all_gather(partial_numerator, 'night'), axis=0)  8.94 us
    dot_general x1, matrix products, shards(): jnp.dot(matrix.reshape(sample_count, local_nights * 3 * sample_count), pa...  8.22 us
    reshape x1, local copies, waits for them, and re-layouts, shards(): padded_slab.reshape(local_nights * 3 * sample_count, baseline_count * 3 *...  6.2 us
    dot_general x1, local copies, waits for them, and re-layouts, shards(): jnp.dot(matrix.reshape(sample_count, local_nights * 3 * sample_count), pa...  6.18 us
  transfers between devices with their start and end apart: 3, of which 3 were waited for; matrix products, arithmetic and copies ran while one was open for 0% of the time, Pallas kernels for 0%

profile of v1, /device:TPU:0, one launch (start us, length us, event | category | flops | bytes accessed | tf_op | source)
XLA Modules:
  0.0 281.6 jit_solution(8261686402865041481)
XLA Ops:
  7.2 0.0 copy-start.2
  7.2 0.0 copy-start.3
  7.2 0.0 copy-start
  7.2 0.0 all-gather.3.cloned.1.call-start
  7.2 0.8 slice_reduce_fusion.1
  8.1 3.0 %fusion.11 = (bf16[1,8,16,1,1536]{4,3,2,1,0:T(2,128)(2,1)S(1)}, bf16[1,8,16,1,1536]{4,3,2,1,0:T(2,128)(2,1)S(1)}) fusion(bf16[1,8,16,2,1536]{4,3,2,1,0:T(2,128)(2,1)} %param.8), kind=kLoop, calls=%fused_computation.30 | loop fusion | bytes 1572864 | tf_op jit(solution)/shard_map/slice | solution.py:37
  11.1 0.0 copy-done.2
  11.1 0.0 copy-done.3
  11.1 0.2 fusion.7
  11.3 0.3 fusion.4
  11.6 0.1 fusion.3
  11.8 0.1 pad_maximum_fusion.1
  11.9 3.9 %collective-permute-start.1 = (bf16[1,8,16,3,1536]{4,2,3,1,0:T(8,128)(2,1)S(1)}, bf16[1,8,16,3,1536]{4,2,3,1,0:T(8,128)(2,1)S(1)}, u32[]{:S(2)}, u32[]{:S(2)}) collective-permute-start(bf16[1,8,16,3,1536]{4,2,3,1,0:T(8,128)(2,1)S(1)} %pad_maximum_fusion.1), channel_id=1, source_target_pairs={{8,0},{16,8},{24,16},{0,24},{9,1},{17,9},{25,17},{1,25},{10,2},{18... | collective-permute-start | bytes 3538952 | tf_op jit(solution)/shard_map/ppermute | solution.py:15
  15.9 0.0 collective-permute-start
  17.2 0.1 maximum_bitcast_fusion
  17.3 0.1 select_reduce_fusion
  17.4 24.9 %collective-permute-done.1 = bf16[1,8,16,3,1536]{4,2,3,1,0:T(8,128)(2,1)S(1)} collective-permute-done((bf16[1,8,16,3,1536]{4,2,3,1,0:T(8,128)(2,1)S(1)}, bf16[1,8,16,3,1536]{4,2,3,1,0:T(8,128)(2,1)S(1)}, u32[]{:S(2)}, u32[]{:S(2)}) %collective-permute-start.1) | collective-permute-done | bytes 1179680 | tf_op jit(solution)/shard_map/ppermute | solution.py:15
  42.2 25.1 %collective-permute-done = bf16[1,8,16,3,1536]{4,2,3,1,0:T(8,128)(2,1)S(1)} collective-permute-done((bf16[1,8,16,3,1536]{4,2,3,1,0:T(8,128)(2,1)S(1)}, bf16[1,8,16,3,1536]{4,2,3,1,0:T(8,128)(2,1)S(1)}, u32[]{:S(2)}, u32[]{:S(2)}) %collective-permute-start) | collective-permute-done | bytes 1179680 | tf_op jit(solution)/shard_map/ppermute | solution.py:14
  67.3 0.4 pad_maximum_fusion
  67.8 5.4 %copy.23 = bf16[1,24,16,3,1536]{4,3,2,1,0:T(4,128)(2,1)} copy(bf16[1,24,16,3,1536]{4,2,3,1,0:T(8,128)(2,1)S(1)} %pad_maximum_fusion) | data formatting | bytes 7077888 | tf_op jit(solution)/shard_map/concatenate | solution.py:16
  73.1 6.2 %reshape.140 = bf16[24,73728]{1,0:T(8,128)(2,1)S(1)} reshape(bf16[1,24,16,3,1536]{4,3,2,1,0:T(4,128)(2,1)} %copy.23) | data formatting | bytes 7077888 | tf_op jit(solution)/shard_map/reshape | solution.py:56
  79.3 6.2 %dot_general.10 = bf16[16,3,1536,24]{2,1,0,3:T(4,128)(2,1)} reshape(bf16[73728,24]{0,1:T(8,128)(2,1)S(1)} %bitcast.27) | data formatting | bytes 7077888 | tf_op jit(solution)/shard_map/dot_general | solution.py:54
  85.5 8.2 %fusion = f32[8,16,3,1536]{3,0,2,1:T(8,128)} fusion(bf16[16,3,1536,24]{2,1,0,3:T(4,128)(2,1)} %dot_general.10, bf16[8,24]{1,0:T(8,128)(2,1)S(1)} %select_reduce_fusion), kind=kOutput, calls=%fused_computation.2 | convolution fusion | flops 28311552 | bytes 5898624 | tf_op jit(solution)/shard_map/dot_general | solution.py:54
  93.7 0.0 all-gather.3.cloned.1.call-update
  93.8 0.0 copy-start.1
  93.8 168.7 %all-gather.3.cloned.1.call-done = f32[64,16,3,1536]{3,0,2,1:T(8,128)} async-done(((f32[8,16,3,1536]{3,0,2,1:T(8,128)}), f32[64,16,3,1536]{3,0,2,1:T(8,128)}) %all-gather.3.cloned.1.call-update) | async-done | bytes 18874384 | tf_op jit(solution)/shard_map/all_gather | solution.py:60
  262.5 8.9 %bitcast_reduce_fusion = f32[8,16,3,1536]{3,0,2,1:T(8,128)S(1)} fusion(f32[64,16,3,1536]{3,0,2,1:T(8,128)} %all-gather.3.cloned.1.call-done), kind=kLoop, calls=%fused_computation | loop fusion | flops 4128768 | bytes 21233664 | tf_op jit(solution)/shard_map/reduce_sum | solution.py:60
  271.5 0.0 copy-done.1
  271.5 0.2 slice_bitcast_fusion
  271.7 0.2 fusion.2
  271.9 1.3 copy.26
  273.2 1.5 copy.25
  (4 shorter events, 0.0 us)
Async XLA Ops:
  7.2 3.9 %copy-start.2 = (f32[1,1536]{1,0:T(1,128)S(1)}, f32[1,1536]{1,0:T(1,128)}, u32[]{:S(2)}) copy-start(f32[1,1536]{1,0:T(1,128)} %param.14) | copy-start | bytes 18436
  7.2 4.0 %copy-start.3 = (s32[1,8]{1,0:T(1,128)S(1)}, s32[1,8]{1,0:T(1,128)}, u32[]{:S(2)}) copy-start(s32[1,8]{1,0:T(1,128)} %param.10) | copy-start | bytes 100
  7.2 4.0 %copy-start = (s32[1,8,16,1536]{3,2,1,0:T(8,128)S(1)}, s32[1,8,16,1536]{3,2,1,0:T(8,128)}, u32[]{:S(2)}) copy-start(s32[1,8,16,1536]{3,2,1,0:T(8,128)} %param.9) | copy-start | bytes 2359300
  7.2 255.3 %all-gather.3.cloned.1.call-start = ((), (), s32[]{:S(2)}) async-start(), calls=%async_computation | async-start | bytes 21233664 | tf_op jit(solution)/shard_map/all_gather | solution.py:60
  11.9 30.3 %collective-permute-start.1 = (bf16[1,8,16,3,1536]{4,2,3,1,0:T(8,128)(2,1)S(1)}, bf16[1,8,16,3,1536]{4,2,3,1,0:T(8,128)(2,1)S(1)}, u32[]{:S(2)}, u32[]{:S(2)}) collective-permute-start(bf16[1,8,16,3,1536]{4,2,3,1,0:T(8,128)(2,1)S(1)} %pad_maximum_fusion.1), channel_id=1, source_target_pairs={{8,0},{16,8},{24,16},{0,24},{9,1},{17,9},{25,17},{1,25},{10,2},{18... | collective-permute-start | bytes 3538952 | tf_op jit(solution)/shard_map/ppermute | solution.py:15
  15.9 51.5 %collective-permute-start = (bf16[1,8,16,3,1536]{4,2,3,1,0:T(8,128)(2,1)S(1)}, bf16[1,8,16,3,1536]{4,2,3,1,0:T(8,128)(2,1)S(1)}, u32[]{:S(2)}, u32[]{:S(2)}) collective-permute-start(bf16[1,8,16,3,1536]{4,2,3,1,0:T(8,128)(2,1)S(1)} %pad_maximum_fusion.1), channel_id=1, source_target_pairs={{0,8},{8,16},{16,24},{24,0},{1,9},{9,17},{17,25},{25,1},{2,10},{10... | collective-permute-start | bytes 3538952 | tf_op jit(solution)/shard_map/ppermute | solution.py:14
  93.8 177.7 %copy-start.1 = (f32[1536]{0:T(1024)S(1)}, f32[1536]{0:T(1024)}, u32[]{:S(2)}) copy-start(f32[1536]{0:T(1024)} %param.15) | copy-start | bytes 18436
Sparse Core Ops, SparseCore 0:
  93.9 168.5 all-gather.2
